TPU v7x, 128 devices: a whole 4x4x4 slice. The times are simulated.
128 devices in a mesh: band: 4 (over y), row: 32 (over x, z, core).
Axes of the slice: x: 4, y: 4, z: 4, core: 2. Of those that a mesh axis runs over, the one named last changes fastest.
Arguments:
- amplitude: bfloat16 [2048, 8192], P('row'), may hold values from 0.5 to 1.5
- seg_map: int32 [2048, 8192], P('row'), may hold values from 0 to 1199, as said below
- seg_box: int32 [4, 1200], replicated, may hold values from 0 to 8191, as said below
- seg_coeffs: float32 [3, 1200], replicated, may hold values from -1 to 1
- probe_freq: int32 [2, 2], replicated, may hold values from 3 to 23
- probe_amp: float32 [2], replicated, may hold values from 0.3 to 0.8
- measured: float32 [8, 256, 4, 2, 256], P('band', 'row'), may hold values from -6 to 6
Outputs:
- gradient: float32 [3, 1200], replicated
Inputs may be any that keep to these rules, and one draw needn't show every extreme that they name: `seg_map`: segments lie in 16 rows of rectangular tiles of whole pupil rows, 75 tiles side by side in each, alternate rows offset by half a tile; segment numbers rise by tile row, then by column; every segment has samples. `seg_box`: the bounds of each segment's samples in seg_map, rows first.
All inputs are finite; a program needn't handle non-finite values.
Results may differ from a plain program's by a relative error of at most 0.0015.
Values may be sent and summed in bfloat16 or wider, within the bound.
A program may use at most 192 MiB of HBM per device.

v0:
```python
import functools
import math

import jax
import jax.numpy as jnp
import ml_dtypes
import numpy as np
from jax import lax
from jax.experimental import pallas as pl
from jax.experimental.pallas import tpu as pltpu
from jax.sharding import PartitionSpec as P

NC = 8192
NR = 2048
M = 256
BANDS = 8
PROBES = 4
SEG = 1200
SROWS = 16
PER_ROW = SEG // SROWS
HALF = M // 2
ROWS = 64
PEERS = 32
OWN = 8
SPREAD = 0.2
SAMPLING = 0.5
MESH = pl.DeviceIdType.MESH
F32 = jnp.float32
BF16 = jnp.bfloat16
SUB = 512
CHUNK = 1024
FOLD = NC // 2
CHUNKS = FOLD // CHUNK
BCHUNK = 1024
TILES = NC // 128
CHIPS = 16
YS = 4
NT = (((1,), (1,)), ((), ()))


def series(fn, top, count):
    cheb = np.polynomial.chebyshev.Chebyshev.interpolate(
        lambda s: fn(np.sqrt(s)), count - 1, domain=[0.0, top * top]
    )
    return [float(v) for v in cheb.convert(kind=np.polynomial.Polynomial).coef]


def sinc(x):
    return np.sinc(x / np.pi)


SIN_PHASE = series(sinc, 3.02, 6)
COS_PHASE = series(np.cos, 3.02, 7)
SIN_WAVE = series(sinc, 0.81, 4)
COS_WAVE = series(np.cos, 0.81, 4)
SIN_TURN = series(lambda x: 2 * np.pi * np.sinc(2 * x), 0.5, 8)
COS_TURN = series(lambda x: np.cos(2 * np.pi * x), 0.5, 8)


def poly(coefs, s):
    total = jnp.full_like(s, coefs[-1])
    for value in coefs[-2::-1]:
        total = total * s + value
    return total


def turn_sincos(turns):
    part = turns - jnp.floor(turns + 0.5)
    square = part * part
    return part * poly(SIN_TURN, square), poly(COS_TURN, square)


def half_tables(coords, order):
    focal = (np.arange(HALF, dtype=np.float32) - np.float32(M / 2) + np.float32(0.5)) * np.float32(SAMPLING)
    base = (np.float32(2.0 * math.pi) * focal)[:, None] * coords[None, :]
    out = []
    for band in range(BANDS):
        ratio = np.float32(1.0) + np.float32(SPREAD) * (
            (np.float32(band) + np.float32(0.5)) / np.float32(BANDS) - np.float32(0.5)
        )
        angle = (base / ratio).astype(np.float64)
        out.append(np.stack([np.cos(angle), np.sin(angle)]).astype(np.float32).astype(ml_dtypes.bfloat16))
    return np.stack(out)


def column_table():
    coords = (np.arange(NC, dtype=np.float32) + np.float32(0.5)) / np.float32(NC) - np.float32(0.5)
    tables = half_tables(coords, 0)[..., :FOLD].reshape(4, 2, 2, HALF, FOLD)
    return tables.transpose(0, 2, 1, 3, 4).reshape(4, 4 * HALF, FOLD)


def row_table():
    coords = (np.arange(NR, dtype=np.float32) + np.float32(0.5)) / np.float32(NC) - np.float32(NR / (2.0 * NC))
    return half_tables(coords, 0).reshape(4, 4 * HALF, NR)


def lane_sign(first, second):
    lane = lax.broadcasted_iota(jnp.int32, (1, 128), 1)
    return jnp.where(lane < 64, F32(first), F32(second))


def iota(shape, dim):
    return lax.broadcasted_iota(jnp.int32, shape, dim)


def wave_setup(row0, freq_ref, amp_ref, roww, colw):
    rows = (iota((ROWS, 128), 0) + row0).astype(F32)
    place = (rows + 0.5) / NC - NR / (2.0 * NC)
    cols = (iota((TILES, 128), 0) * 128 + iota((TILES, 128), 1)).astype(F32)
    across = (cols + 0.5) / NC - 0.5
    for j in range(2):
        s, c = turn_sincos(place * freq_ref[j, 1].astype(F32))
        roww[2 * j] = s * amp_ref[j]
        roww[2 * j + 1] = c * amp_ref[j]
        s, c = turn_sincos(across * freq_ref[j, 0].astype(F32))
        colw[2 * j] = s
        colw[2 * j + 1] = c


def wave_sincos(j, rows, tile, roww, colw):
    one = roww[2 * j + 1, rows, :] * colw[2 * j, pl.ds(tile, 1), :]
    two = roww[2 * j, rows, :] * colw[2 * j + 1, pl.ds(tile, 1), :]
    out = []
    for wave in (two + one, two - one):
        square = wave * wave
        out.append((wave * poly(SIN_WAVE, square), poly(COS_WAVE, square)))
    return out


def lanes(index, width):
    return pl.ds(pl.multiple_of(index * width, width), width)


def segment_setup(row0, box_ref, coef_ref, seg, flat, tabs, rowt, base, pick):
    flat[...] = jnp.zeros_like(flat)
    flat[0:4, 0:SEG] = box_ref[...].astype(F32)
    flat[4:7, 0:SEG] = coef_ref[...]
    lane = iota((8, 128), 1)
    for t in range(SROWS):
        first, off = divmod(PER_ROW * t, 128)
        one = flat[:, 128 * first : 128 * first + 128]
        if off:
            two = flat[:, 128 * first + 128 : 128 * first + 256]
            one = jnp.where(lane < 128 - off, pltpu.roll(one, 128 - off, 1), pltpu.roll(two, 128 - off, 1))
        tabs[t] = one
    column = seg[:, 0:1]
    trow = jnp.zeros((ROWS, 1), jnp.int32)
    for m in range(1, SROWS):
        trow = trow + (column >= PER_ROW * m).astype(jnp.int32)
    trow = jnp.broadcast_to(trow, (ROWS, 128))
    base[...] = trow * PER_ROW
    rows = (iota((ROWS, 128), 0) + row0).astype(F32)
    alpha, beta, middle, down_all = [jnp.zeros((ROWS, 128), F32) for _ in range(4)]
    for t in range(SROWS):
        r0, r1, c0, c1 = [tabs[t, q : q + 1, :] for q in range(4)]
        piston, tip, tilt = [tabs[t, q : q + 1, :] for q in range(4, 7)]
        here = trow == t
        down = (rows - 0.5 * (r0 + r1)) / (0.5 * (r1 - r0 + 1.0))
        alpha = jnp.where(here, piston + tilt * down, alpha)
        beta = jnp.where(here, tip / (0.5 * (c1 - c0 + 1.0)), beta)
        middle = jnp.where(here, 0.5 * (c0 + c1), middle)
        down_all = jnp.where(here, down, down_all)
    rowt[0] = alpha
    rowt[1] = beta
    rowt[2] = middle
    lane = iota((ROWS, 128), 1)
    down_all = jnp.broadcast_to(down_all[:, 0:1], (ROWS, 128))
    high = down_all.astype(BF16).astype(F32)
    which = jnp.where(lane < 16, 1.0, jnp.where(lane < 32, high, jnp.where(lane < 48, down_all - high, 0.0)))
    chosen = jnp.where(lax.rem(lane, 16) == trow, which, 0.0)
    pick[...] = jnp.concatenate([chosen, chosen], axis=0).T.astype(BF16)


def fields(j, chunk, ebuf, amp, seg, rowt, base, roww, colw, pbuf):
    lane = iota((32, 128), 1)
    for lt in range(SUB // 128):
        tile = chunk * (SUB // 128) + lt
        cols = slice(128 * lt, 128 * lt + 128)
        for rh in range(2):
            rows = slice(32 * rh, 32 * rh + 32)
            both = []
            for side in range(2):
                at = tile if side == 0 else TILES - 1 - tile
                wide = lanes(at, 128)
                if j == 0:
                    cf = (lane + at * 128).astype(F32)
                    idx = seg[rows, wide] - base[rows, :]
                    a = jnp.take_along_axis(rowt[0, rows, :], idx, axis=1)
                    b = jnp.take_along_axis(rowt[1, rows, :], idx, axis=1)
                    m = jnp.take_along_axis(rowt[2, rows, :], idx, axis=1)
                    phase = a + b * (cf - m)
                    mag = amp[rows, wide].astype(F32)
                    if side == 1:
                        phase = jnp.take_along_axis(phase, 127 - lane, axis=1)
                        mag = jnp.take_along_axis(mag, 127 - lane, axis=1)
                    square = phase * phase
                    pr = mag * poly(COS_PHASE, square)
                    pi = mag * (phase * poly(SIN_PHASE, square))
                    pbuf[0, rows, wide] = pr
                    pbuf[1, rows, wide] = pi
                else:
                    pr = pbuf[0, rows, wide]
                    pi = pbuf[1, rows, wide]
                both.append((pr, pi))
            waves = wave_sincos(j, rows, tile, roww, colw)
            for t in range(2):
                f, g = waves[0][1 - t], waves[1][1 - t]
                for o in range(2):
                    one, two = both[0][o] * f, both[1][o] * g
                    at = 128 * t + 64 * o + 32 * rh
                    ebuf[at : at + 32, cols] = (one + two).astype(BF16)
                    ebuf[256 + at : 288 + at, cols] = (one - two).astype(BF16)


def add_dots(acc, ctab, index, ebuf):
    for part in range(2):
        rows = slice(256 * part, 256 * part + 256)
        acc[rows, :] += lax.dot_general(ctab[rows, lanes(index, SUB)], ebuf[rows, :], NT,
                                        preferred_element_type=F32)


def column_sums(acc, pay, ysc):
    plus = lane_sign(1.0, -1.0)
    for b in range(2):
        parts = []
        for t in range(2):
            cols = slice(128 * t, 128 * t + 128)
            c = acc[128 * b : 128 * b + 128, cols]
            s = plus * pltpu.roll(acc[256 + 128 * b : 384 + 128 * b, cols], 64, 1)
            parts.append((c + s, c - s))
        for side in range(2):
            even = parts[0][side]
            odd = plus * pltpu.roll(parts[1][side], 64, 1)
            ysc[side, b, :, 0:128] = even - odd
            ysc[side, b, :, 128:256] = even + odd
    for d in range(PEERS // 2):
        for side in range(2):
            to = d if side == 0 else PEERS - 1 - d
            pay[to] = jnp.concatenate(
                [ysc[side, b, OWN * d : OWN * d + OWN, :] for b in range(2)], axis=0
            ).astype(BF16)


def focal_part(j, normf, recv, hpay, lhs, hs, ms, table):
    low = iota((16, 128), 1) < 64

    def gather(s4, carry):
        for k in range(4):
            s = s4 * 4 + k
            cols = lanes(s, 128)
            for q in range(2):
                one = recv[2 * s, :, 128 * q : 128 * q + 128].astype(F32)
                two = recv[2 * s + 1, :, 128 * q : 128 * q + 128].astype(F32)
                re = jnp.where(low, one, pltpu.roll(two, 64, 1))
                im = jnp.where(low, pltpu.roll(one, 64, 1), two)
                for b in range(2):
                    lhs[b, 16 * q : 16 * q + 8, cols] = re[8 * b : 8 * b + 8]
                    lhs[b, 16 * q + 8 : 16 * q + 16, cols] = im[8 * b : 8 * b + 8]
        return carry
    lax.fori_loop(0, PEERS // 8, gather, 0)

    for b in range(2):
        here = table[256 * b : 256 * b + 256, :]
        parts = lax.dot_general(lhs[b].astype(BF16), here, NT, preferred_element_type=F32)
        rows = []
        for q in range(2):
            re, im = parts[16 * q : 16 * q + 8], parts[16 * q + 8 : 16 * q + 16]
            pieces = []
            for o, (c, s) in enumerate(((re[:, :HALF], im[:, HALF:]), (im[:, :HALF], -re[:, HALF:]))):
                want = pl.ds(b * 64 + 4 * j + 2 * q + o, 8, stride=8)
                one = (c + s) * normf - ms[0, want, :]
                two = (c - s) * normf - ms[1, want, :]
                pieces.append((one + two, one - two))
            (re_e, re_o), (im_e, im_o) = pieces
            rows.append(jnp.concatenate([re_e, -im_o], axis=1))
            rows.append(jnp.concatenate([im_e, re_o], axis=1))
        left = jnp.concatenate(rows, axis=0).astype(BF16)
        hs[b] = jnp.dot(left, here, preferred_element_type=F32)

    low8 = iota((8, 128), 1) < 64

    def spread(s4, carry):
        for k in range(4):
            s = s4 * 4 + k
            cols = lanes(s, 128)
            for q in range(2):
                first, second = [], []
                for b in range(2):
                    re = hs[b, 16 * q : 16 * q + 8, cols]
                    im = hs[b, 16 * q + 8 : 16 * q + 16, cols]
                    first.append(jnp.where(low8, re, pltpu.roll(im, 64, 1)))
                    second.append(jnp.where(low8, pltpu.roll(re, 64, 1), im))
                hpay[2 * s, :, 128 * q : 128 * q + 128] = jnp.concatenate(first, axis=0).astype(BF16)
                hpay[2 * s + 1, :, 128 * q : 128 * q + 128] = jnp.concatenate(second, axis=0).astype(BF16)
        return carry
    lax.fori_loop(0, PEERS // 8, spread, 0)


def hidden_left(j, hid, left, leftt):
    minus = lane_sign(-1.0, 1.0)
    for d in range(PEERS // 2):
        here = hid[d].astype(F32)
        there = hid[PEERS - 1 - d].astype(F32)
        even, odd = here + there, here - there
        e = [even[:, 128 * t : 128 * t + 128] for t in range(2)]
        o = [odd[:, 128 * t : 128 * t + 128] for t in range(2)]
        for t in range(2):
            cols = slice(128 * t, 128 * t + 128)
            es = e[0] + e[1] if t == 0 else e[0] - e[1]
            os = o[0] + o[1] if t == 0 else o[0] - o[1]
            os = minus * pltpu.roll(os, 64, 1)
            for b in range(2):
                left[128 * b + 8 * d : 128 * b + 8 * d + 8, cols] = es[8 * b : 8 * b + 8]
                left[256 + 128 * b + 8 * d : 264 + 128 * b + 8 * d, cols] = os[8 * b : 8 * b + 8]
    leftt[256 * j : 256 * j + 256, :] = left[...].T.astype(BF16)


def weights(lt, piece, gbuf, roww, colw, pbuf, wst):
    for lh in range(2):
        tile = piece * 2 + lh
        gc = slice(128 * lh, 128 * lh + 128)
        for rh in range(2):
            rows = slice(32 * rh, 32 * rh + 32)
            zr, zi = [0.0, 0.0], [0.0, 0.0]
            for j in range(2):
                waves = wave_sincos(j, rows, tile, roww, colw)
                at = [256 * j + 64 * n + 32 * rh for n in range(4)]
                even = [gbuf[lt, 0, x : x + 32, gc] for x in at]
                odd = [gbuf[lt, 1, x : x + 32, gc] for x in at]
                for side in range(2):
                    g = [e + o if side == 0 else e - o for e, o in zip(even, odd)]
                    sw, cw = waves[side]
                    zr[side] = zr[side] + (cw * g[0] + sw * g[3])
                    zi[side] = zi[side] + (cw * g[1] - sw * g[2])
            for side in range(2):
                wide = lanes(tile if side == 0 else TILES - 1 - tile, 128)
                w = pbuf[0, rows, wide] * zi[side] - pbuf[1, rows, wide] * zr[side]
                high = w.astype(BF16)
                wst[32 * rh : 32 * rh + 32, wide] = high
                wst[64 + 32 * rh : 96 + 32 * rh, wide] = (w - high.astype(F32)).astype(BF16)


def backward(chunk, leftt, table, gbuf, roww, colw, pbuf, wst):
    count = BCHUNK // 256
    for lt in range(count + 1):
        piece = chunk * count + lt
        if lt < count:
            for part in range(2):
                ks = slice(256 * part, 256 * part + 256)
                gbuf[lt, part] = jnp.dot(leftt[:, ks], table[ks, lanes(piece, 256)], preferred_element_type=F32)
        if lt > 0:
            weights(lt - 1, piece - 1, gbuf, roww, colw, pbuf, wst)


def prefix_weights(at, col):
    to = jnp.where(col < 256, lax.rem(col, 128), 127)
    weight = jnp.where(lax.rem(col, 256) < 128, 1.0, at.astype(F32))
    return jnp.where(at <= to, weight, 0.0).astype(BF16)


def segment_sums(tabs, wst, pick, ulow, tris, pre0, pre1, sbuf, pack):
    row, col = iota((256, 512), 0), iota((256, 512), 1)
    at = lax.rem(row, 128)
    for side in range(2):
        tris[side] = prefix_weights(at if side == 0 else 127 - at, col)
    c0 = jnp.concatenate([tabs[t, 2:3, :] for t in range(SROWS)], axis=0)
    c1 = jnp.concatenate([tabs[t, 3:4, :] for t in range(SROWS)], axis=0)
    tile0 = jnp.floor(c0 * (1.0 / 128.0))
    tile1 = jnp.floor(c1 * (1.0 / 128.0))
    in0 = c0 - 128.0 * tile0 - 1.0
    idx0 = jnp.maximum(in0, 0.0).astype(jnp.int32)
    idx1 = (c1 - 128.0 * tile1).astype(jnp.int32)
    some = in0 >= 0.0
    middle = 0.5 * (c0 + c1)

    def row_sums(k, carry):
        u = jnp.dot(pick[0:48, :], wst[:, lanes(k, 1024)], preferred_element_type=F32)
        parts = []
        for lt in range(8):
            gc = slice(128 * lt, 128 * lt + 128)
            parts += [u[0:16, gc], u[16:32, gc] + u[32:48, gc]]
        u = jnp.concatenate(parts, axis=0)
        high = u.astype(BF16)
        low = (u - high.astype(F32)).astype(BF16)
        ulow[pl.ds(pl.multiple_of(k * 256, 256), 256), :] = jnp.concatenate([high, low], axis=1)
        return carry
    lax.fori_loop(0, TILES // 8, row_sums, 0, unroll=4)

    def prefix(k, pre):
        rows = pl.ds(pl.multiple_of(k * 256, 256), 256)
        pre[...] = jnp.dot(ulow[rows, :], tris[k // (TILES // 16)], preferred_element_type=F32)

    def edges(k, pre, sums):
        sums = list(sums)
        for lt in range(8):
            tile = (k * 8 + lt).astype(F32)
            last1, last0 = tile1 == tile, tile0 == tile
            over1, over0 = tile1 > tile, tile0 > tile
            diffs = []
            for half, at in ((0, 0), (1, 0), (0, 16)):
                rows = slice(32 * lt + at, 32 * lt + at + 16)
                a = pre[rows, 128 * half : 128 * half + 128]
                whole = pre[rows, 128 * half + 256 : 128 * half + 384]
                g1 = jnp.take_along_axis(a, idx1, axis=1)
                g0 = jnp.where(some, jnp.take_along_axis(a, idx0, axis=1), 0.0)
                upto1 = jnp.where(last1, g1, jnp.where(over1, whole, 0.0))
                upto0 = jnp.where(last0, g0, jnp.where(over0, whole, 0.0))
                diffs.append(upto1 - upto0)
            sums[0] = sums[0] + diffs[0]
            sums[1] = sums[1] + (diffs[1] + (128.0 * tile - middle) * diffs[0])
            sums[2] = sums[2] + diffs[2]
        return tuple(sums)

    pre1[...] = jnp.zeros_like(pre1)

    def pair(m, sums):
        prefix(2 * m, pre0)
        sums = edges(2 * m - 1, pre1, sums)
        prefix(2 * m + 1, pre1)
        return edges(2 * m, pre0, sums)
    zero = jnp.zeros((SROWS, 128), F32)
    sums = lax.fori_loop(0, TILES // 16, pair, (zero, zero, zero))
    s0, s1, s2 = edges(jnp.int32(TILES // 8 - 1), pre1, sums)
    keep = iota((SROWS, 128), 1) < PER_ROW
    s1 = s1 / (0.5 * (c1 - c0 + 1.0))
    s0, s1, s2 = [jnp.where(keep, v, 0.0) for v in (s0, s1, s2)]
    sbuf[...] = jnp.zeros_like(sbuf)
    for t in range(SROWS):
        sbuf[t, 0:1, :] = s0[t : t + 1]
        sbuf[t, 1:2, :] = s1[t : t + 1]
        sbuf[t, 2:3, :] = s2[t : t + 1]

    packed = [jnp.zeros((8, 128), F32) for _ in range(10)]
    lane = iota((8, 128), 1)
    for t in range(SROWS):
        first, off = divmod(PER_ROW * t, 128)
        turned = pltpu.roll(sbuf[t], off, 1) if off else sbuf[t]
        packed[first] = packed[first] + jnp.where(lane >= off, turned, 0.0)
        if off + PER_ROW > 128:
            packed[first + 1] = packed[first + 1] + jnp.where(lane < off, turned, 0.0)
    for q in range(3):
        for k in range(10):
            p, r = divmod(q * 10 + k, 8)
            pack[p, r : r + 1, :] = packed[k][q : q + 1, :]
    pack[3, 6:8, :] = jnp.zeros((2, 128), F32)


def remote(src, dst, ssem, rsem, where):
    return pltpu.make_async_remote_copy(src_ref=src, dst_ref=dst, send_sem=ssem, recv_sem=rsem,
                                        device_id=where, device_id_type=MESH)


def each(count, fn):
    def step(o, carry):
        fn(o)
        return carry
    lax.fori_loop(1, count, step, 0)


def kernel(normf, scale, amp_hbm, seg_hbm, box_hbm, coef_hbm, freq_ref, pamp_ref, meas_hbm, ctab_hbm, rtab_hbm,
           out_ref, box_ref, coef_ref, meas_ref, amp, seg, ctab, rtab, flat, tabs, rowt, base, pick, roww, colw, pbuf, eb0, eb1, acc, ysc,
           pay, recv, lhs, hs, ms, hpay, hid, left, leftt, gbuf, wst, ulow, tris, pre0, pre1, sbuf, pack,
           got_a, mine_b, got_b, mine_c, got_c, lsem, tsem, osem, ssem, rsem, asem, bsem, csem):
    band = lax.axis_index("band")
    me = lax.axis_index("row")
    core = lax.rem(me, 2)
    chip = me // 2
    row0 = me * ROWS

    def loads(i):
        cols, mirror = lanes(i, CHUNK), lanes(2 * CHUNKS - 1 - i, CHUNK)
        return [pltpu.make_async_copy(seg_hbm.at[:, cols], seg.at[:, cols], lsem.at[0, i]),
                pltpu.make_async_copy(seg_hbm.at[:, mirror], seg.at[:, mirror], lsem.at[1, i]),
                pltpu.make_async_copy(amp_hbm.at[:, cols], amp.at[:, cols], lsem.at[2, i]),
                pltpu.make_async_copy(amp_hbm.at[:, mirror], amp.at[:, mirror], lsem.at[3, i]),
                pltpu.make_async_copy(ctab_hbm.at[band, :, cols], ctab.at[:, cols], lsem.at[4, i])]

    def start_loads(i, carry):
        for copy in loads(i):
            copy.start()
        return carry
    small = [pltpu.make_async_copy(box_hbm, box_ref, osem.at[0]),
             pltpu.make_async_copy(coef_hbm, coef_ref, osem.at[1]),
             pltpu.make_async_copy(meas_hbm, meas_ref, osem.at[2])]
    small[0].start()
    small[1].start()
    lax.fori_loop(0, CHUNKS, start_loads, 0)
    small[2].start()
    table_copy = pltpu.make_async_copy(rtab_hbm.at[band], rtab, tsem)
    table_copy.start()

    barrier = pltpu.get_barrier_semaphore()

    def greet(where):
        pl.semaphore_signal(barrier, inc=1, device_id=where, device_id_type=MESH)
    each(PEERS, lambda o: greet((band, lax.rem(me + o, PEERS))))
    for o in range(1, YS):
        for c in range(2):
            greet((lax.rem(band + o, YS), chip * 2 + c))

    wave_setup(row0, freq_ref, pamp_ref, roww, colw)
    def send(j, source, target):
        def one(o):
            peer = lax.rem(me + o, PEERS)
            remote(source.at[j, peer], target.at[j, me], ssem.at[j, peer], rsem.at[j, me], (band, peer)).start()
        each(PEERS, one)

    def await_all(j, source, target):
        def one(o):
            peer = lax.rem(me + o, PEERS)
            remote(source.at[j, peer], target.at[j, peer], ssem.at[j, peer], rsem.at[j, peer], (band, peer)).wait()
        each(PEERS, one)

    for j in range(2):
        acc[...] = jnp.zeros_like(acc)
        eb1[...] = jnp.zeros_like(eb1)

        def forward(i, carry):
            if j == 0:
                for copy in loads(i):
                    copy.wait()

                @pl.when(i == 0)
                def _():
                    small[0].wait()
                    small[1].wait()
                    segment_setup(row0, box_ref, coef_ref, seg, flat, tabs, rowt, base, pick)
            before = jnp.maximum(2 * i - 1, 0)
            fields(j, 2 * i, eb0, amp, seg, rowt, base, roww, colw, pbuf)
            add_dots(acc, ctab, before, eb1)
            fields(j, 2 * i + 1, eb1, amp, seg, rowt, base, roww, colw, pbuf)
            add_dots(acc, ctab, 2 * i, eb0)
            return carry
        lax.fori_loop(0, CHUNKS, forward, 0)
        add_dots(acc, ctab, FOLD // SUB - 1, eb1)
        column_sums(acc, pay.at[j], ysc)
        if j == 0:
            pl.semaphore_wait(barrier, PEERS - 1 + 2 * (YS - 1))
        send(j, pay, recv)
        recv[j, me] = pay[j, me]

    small[2].wait()
    for b in range(2):
        for v in range(OWN):
            source = jnp.where(me < PEERS // 2, v, OWN - 1 - v)
            for k in range(PROBES):
                at = b * 64 + 8 * v + 2 * k
                ms[0, at : at + 2, :] = meas_ref[b, source, k, :, :HALF]
                ms[1, at : at + 2, :] = meas_ref[b, source, k, :, HALF:]
    flip = (iota((128, 128), 0) + iota((128, 128), 1) == 127).astype(F32)
    ms[1] = jnp.dot(ms[1], flip, precision=lax.Precision.HIGHEST, preferred_element_type=F32)
    table_copy.wait()
    for j in range(2):
        await_all(j, pay, recv)
        focal_part(j, normf, recv.at[j], hpay.at[j], lhs, hs, ms, rtab)
        def one(o):
            peer = lax.rem(me + o, PEERS)
            remote(hpay.at[j, peer], hid.at[j, me], ssem.at[2 + j, peer], rsem.at[2 + j, me], (band, peer)).start()
        each(PEERS, one)
        hid[j, me] = hpay[j, me]

    for j in range(2):
        def done(o):
            peer = lax.rem(me + o, PEERS)
            remote(hpay.at[j, peer], hid.at[j, peer], ssem.at[2 + j, peer], rsem.at[2 + j, peer],
                   (band, peer)).wait()
        each(PEERS, done)
        hidden_left(j, hid.at[j], left, leftt)

    def back(i, carry):
        backward(i, leftt, ctab, gbuf, roww, colw, pbuf, wst)
        return carry
    lax.fori_loop(0, FOLD // BCHUNK, back, 0)

    segment_sums(tabs, wst, pick, ulow, tris, pre0, pre1, sbuf, pack)

    near = band * 2 + core

    def near_copy(o, slot):
        peer = lax.rem(near + o, 2 * YS)
        to = peer // 2
        at = near if slot == "mine" else peer
        return remote(pack.at[to], got_a.at[at], asem.at[0, peer], asem.at[1, at],
                      (to, chip * 2 + lax.rem(peer, 2)))
    each(2 * YS, lambda o: near_copy(o, "mine").start())
    got_a[near] = pack[band]
    each(2 * YS, lambda o: near_copy(o, "peer").wait())
    total = got_a[0]
    for k in range(1, 2 * YS):
        total = total + got_a[k]
    mine_b[...] = total

    def far_copy(o, slot):
        peer = lax.rem(chip + o, CHIPS)
        at = chip if slot == "mine" else peer
        return remote(mine_b, got_b.at[at], bsem.at[0, peer], bsem.at[1, at], (band, peer * 2 + core))
    each(CHIPS, lambda o: far_copy(o, "mine").start())
    got_b[chip] = mine_b[...]
    each(CHIPS, lambda o: far_copy(o, "peer").wait())
    total = got_b[0]
    for k in range(1, CHIPS):
        total = total + got_b[k]
    mine_c[...] = total * scale

    def share_copy(o, slot):
        peer = lax.rem(band + o, YS)
        at = band if slot == "mine" else peer
        return remote(mine_c, got_c.at[at], csem.at[0, peer], csem.at[1, at], (peer, me))
    each(YS, lambda o: share_copy(o, "mine").start())
    got_c[band] = mine_c[...]
    each(YS, lambda o: share_copy(o, "peer").wait())
    for q in range(3):
        for k in range(10):
            p, r = divmod(q * 10 + k, 8)
            width = min(128, SEG - 128 * k)
            out_ref[q : q + 1, 128 * k : 128 * k + width] = got_c[p, r : r + 1, :width]


VM = pl.BlockSpec(memory_space=pltpu.VMEM)
SM = pl.BlockSpec(memory_space=pltpu.SMEM)
HBM = pl.BlockSpec(memory_space=pl.ANY)
LIMIT = 60 * 1024 * 1024


def solution(mesh):
    ctable = jnp.asarray(column_table())
    rtable = jnp.asarray(row_table())
    root = math.sqrt(NR * NC)

    def body(amplitude, seg_map, seg_box, seg_coeffs, probe_freq, probe_amp, measured):
        dma = pltpu.SemaphoreType.DMA
        return pl.pallas_call(
            functools.partial(kernel, 1.0 / root, 2.0 / root / (BANDS * PROBES)),
            in_specs=[HBM, HBM, HBM, HBM, SM, SM, HBM, HBM, HBM],
            out_specs=VM,
            out_shape=jax.ShapeDtypeStruct((3, SEG), F32),
            scratch_shapes=[
                pltpu.VMEM((4, SEG), jnp.int32),
                pltpu.VMEM((3, SEG), F32),
                pltpu.VMEM((2, OWN, PROBES, 2, M), F32),
                pltpu.VMEM((ROWS, NC), BF16),
                pltpu.VMEM((ROWS, NC), jnp.int32),
                pltpu.VMEM((4 * HALF, FOLD), BF16),
                pltpu.VMEM((4 * HALF, NR), BF16),
                pltpu.VMEM((8, 1280), F32),
                pltpu.VMEM((SROWS, 8, 128), F32),
                pltpu.VMEM((3, ROWS, 128), F32),
                pltpu.VMEM((ROWS, 128), jnp.int32),
                pltpu.VMEM((128, 128), BF16),
                pltpu.VMEM((4, ROWS, 128), F32),
                pltpu.VMEM((4, TILES, 128), F32),
                pltpu.VMEM((2, ROWS, NC), F32),
                pltpu.VMEM((512, SUB), BF16),
                pltpu.VMEM((512, SUB), BF16),
                pltpu.VMEM((4 * HALF, 256), F32),
                pltpu.VMEM((2, 2, HALF, 256), F32),
                pltpu.VMEM((2, PEERS, 16, 256), BF16),
                pltpu.VMEM((2, PEERS, 16, 256), BF16),
                pltpu.VMEM((2, 32, NR), F32),
                pltpu.VMEM((2, 32, NR), F32),
                pltpu.VMEM((2, 128, HALF), F32),
                pltpu.VMEM((2, PEERS, 16, 256), BF16),
                pltpu.VMEM((2, PEERS, 16, 256), BF16),
                pltpu.VMEM((4 * HALF, 256), F32),
                pltpu.VMEM((512, 4 * HALF), BF16),
                pltpu.VMEM((BCHUNK // 256, 2, 512, 256), F32),
                pltpu.VMEM((128, NC), BF16),
                pltpu.VMEM((TILES * 32, 256), BF16),
                pltpu.VMEM((2, 256, 512), BF16),
                pltpu.VMEM((256, 512), F32),
                pltpu.VMEM((256, 512), F32),
                pltpu.VMEM((SROWS, 8, 128), F32),
                pltpu.VMEM((4, 8, 128), F32),
                pltpu.VMEM((2 * YS, 8, 128), F32),
                pltpu.VMEM((8, 128), F32),
                pltpu.VMEM((CHIPS, 8, 128), F32),
                pltpu.VMEM((8, 128), F32),
                pltpu.VMEM((YS, 8, 128), F32),
                dma((5, CHUNKS)),
                dma,
                dma((3,)),
                dma((4, PEERS)),
                dma((4, PEERS)),
                dma((2, 2 * YS)),
                dma((2, CHIPS)),
                dma((2, YS)),
            ],
            compiler_params=pltpu.CompilerParams(collective_id=0, has_side_effects=True, vmem_limit_bytes=LIMIT),
            name="gradient",
        )(amplitude, seg_map, seg_box, seg_coeffs, probe_freq, probe_amp, measured, ctable, rtable)

    in_specs = (P("row", None), P("row", None), P(), P(), P(), P(), P("band", "row", None, None, None))
    return jax.shard_map(body, mesh=mesh, in_specs=in_specs, out_specs=P(), check_vma=False)
```

profile of v0, /device:TPU:0, one launch (start us, length us, event | category | flops | bytes accessed | tf_op | source)
XLA Modules:
  0.0 63.6 jit_solution(6620991029268062350)
XLA Ops:
  0.0 62.2 %gradient.1 = f32[3,1200]{1,0:T(4,128)} custom-call(bf16[64,8192]{1,0:T(8,128)(2,1)} %amp_hbm.1, s32[64,8192]{1,0:T(8,128)} %seg_hbm.1, s32[4,1200]{1,0:T(4,128)} %box_hbm.1, f32[3,1200]{1,0:T(4,128)} %coef_hbm.1, s32[2,2]{1,0:T(2,128)} %freq_ref.1, f32[2]{0:T(128)} %pamp_ref.1, f32[2,8,4,2,256]{4,3,2,1,0:T(2,128)} %meas_hbm.1, ...), custom_call_target="tpu_custom_call" | custom-call | tf_op jit(solution)/shard_map/gradient/pallas_call | solution.py:632
  62.2 1.3 %copy.11 = f32[3,1200]{1,0:T(4,128)} copy(f32[3,1200]{1,0:T(4,128)} %gradient.1) | data formatting | bytes 28800
where the time goes:
time: 63.7 us; the launch traced here: 63.6 us
  Pallas kernels  62.2 us (98%)
  local copies, waits for them, and re-layouts  1.34 us (2%)
    pallas_call x1, Pallas kernels, body(): pl.pallas_call(functools.partial(kernel, 1.0 / root, 2.0 / root / (BANDS...  62.2 us
    unnamed x1, local copies, waits for them, and re-layouts  1.34 us

commit v1 on v0

--- a/solution.py
+++ b/solution.py
@@ -27,6 +27,7 @@
 MESH = pl.DeviceIdType.MESH
 F32 = jnp.float32
 BF16 = jnp.bfloat16
+STEP = 64
 SUB = 512
 CHUNK = 1024
 FOLD = NC // 2
@@ -171,13 +172,13 @@
     pick[...] = jnp.concatenate([chosen, chosen], axis=0).T.astype(BF16)
 
 
-def fields(j, chunk, ebuf, amp, seg, rowt, base, roww, colw, pbuf):
-    lane = iota((32, 128), 1)
+def fields(j, chunk, ebuf, amp, seg, rowt, base, roww, colw, pbuf, wbuf):
+    lane = iota((STEP, 128), 1)
     for lt in range(SUB // 128):
         tile = chunk * (SUB // 128) + lt
         cols = slice(128 * lt, 128 * lt + 128)
-        for rh in range(2):
-            rows = slice(32 * rh, 32 * rh + 32)
+        for rh in range(ROWS // STEP):
+            rows = slice(STEP * rh, STEP * rh + STEP)
             both = []
             for side in range(2):
                 at = tile if side == 0 else TILES - 1 - tile
@@ -203,13 +204,17 @@
                     pi = pbuf[1, rows, wide]
                 both.append((pr, pi))
             waves = wave_sincos(j, rows, tile, roww, colw)
+            for side in range(2):
+                wide = lanes(tile if side == 0 else TILES - 1 - tile, 128)
+                wbuf[2 * j, rows, wide] = waves[side][0]
+                wbuf[2 * j + 1, rows, wide] = waves[side][1]
             for t in range(2):
                 f, g = waves[0][1 - t], waves[1][1 - t]
                 for o in range(2):
                     one, two = both[0][o] * f, both[1][o] * g
-                    at = 128 * t + 64 * o + 32 * rh
-                    ebuf[at : at + 32, cols] = (one + two).astype(BF16)
-                    ebuf[256 + at : 288 + at, cols] = (one - two).astype(BF16)
+                    at = 128 * t + 64 * o + STEP * rh
+                    ebuf[at : at + STEP, cols] = (one + two).astype(BF16)
+                    ebuf[256 + at : 256 + at + STEP, cols] = (one - two).astype(BF16)
 
 
 def add_dots(acc, ctab, index, ebuf):
@@ -315,7 +320,7 @@
     leftt[256 * j : 256 * j + 256, :] = left[...].T.astype(BF16)
 
 
-def weights(lt, piece, gbuf, roww, colw, pbuf, wst):
+def weights(lt, piece, gbuf, wbuf, pbuf, wst):
     for lh in range(2):
         tile = piece * 2 + lh
         gc = slice(128 * lh, 128 * lh + 128)
@@ -323,13 +328,13 @@
             rows = slice(32 * rh, 32 * rh + 32)
             zr, zi = [0.0, 0.0], [0.0, 0.0]
             for j in range(2):
-                waves = wave_sincos(j, rows, tile, roww, colw)
                 at = [256 * j + 64 * n + 32 * rh for n in range(4)]
                 even = [gbuf[lt, 0, x : x + 32, gc] for x in at]
                 odd = [gbuf[lt, 1, x : x + 32, gc] for x in at]
                 for side in range(2):
                     g = [e + o if side == 0 else e - o for e, o in zip(even, odd)]
-                    sw, cw = waves[side]
+                    wide = lanes(tile if side == 0 else TILES - 1 - tile, 128)
+                    sw, cw = wbuf[2 * j, rows, wide], wbuf[2 * j + 1, rows, wide]
                     zr[side] = zr[side] + (cw * g[0] + sw * g[3])
                     zi[side] = zi[side] + (cw * g[1] - sw * g[2])
             for side in range(2):
@@ -340,7 +345,7 @@
                 wst[64 + 32 * rh : 96 + 32 * rh, wide] = (w - high.astype(F32)).astype(BF16)
 
 
-def backward(chunk, leftt, table, gbuf, roww, colw, pbuf, wst):
+def backward(chunk, leftt, table, gbuf, wbuf, pbuf, wst):
     count = BCHUNK // 256
     for lt in range(count + 1):
         piece = chunk * count + lt
@@ -349,28 +354,34 @@
                 ks = slice(256 * part, 256 * part + 256)
                 gbuf[lt, part] = jnp.dot(leftt[:, ks], table[ks, lanes(piece, 256)], preferred_element_type=F32)
         if lt > 0:
-            weights(lt - 1, piece - 1, gbuf, roww, colw, pbuf, wst)
-
-
-def prefix_weights(at, col):
-    to = jnp.where(col < 256, lax.rem(col, 128), 127)
-    weight = jnp.where(lax.rem(col, 256) < 128, 1.0, at.astype(F32))
-    return jnp.where(at <= to, weight, 0.0).astype(BF16)
+            weights(lt - 1, piece - 1, gbuf, wbuf, pbuf, wst)
+
+
+def prefix_weights(tris):
+    row, lane = iota((128, 128), 0), iota((128, 128), 1)
+    for side in range(2):
+        at = row if side == 0 else 127 - row
+        weight = at.astype(F32)
+        some = at <= lane
+        one = jnp.where(some, 1.0, 0.0).astype(BF16)
+        two = jnp.where(some, weight, 0.0).astype(BF16)
+        three = jnp.ones((128, 128), BF16)
+        four = weight.astype(BF16)
+        for half in range(2):
+            for q, part in enumerate((one, two, three, four)):
+                tris[side, 128 * half : 128 * half + 128, 128 * q : 128 * q + 128] = part
 
 
 def segment_sums(tabs, wst, pick, ulow, tris, pre0, pre1, sbuf, pack):
-    row, col = iota((256, 512), 0), iota((256, 512), 1)
-    at = lax.rem(row, 128)
-    for side in range(2):
-        tris[side] = prefix_weights(at if side == 0 else 127 - at, col)
     c0 = jnp.concatenate([tabs[t, 2:3, :] for t in range(SROWS)], axis=0)
     c1 = jnp.concatenate([tabs[t, 3:4, :] for t in range(SROWS)], axis=0)
-    tile0 = jnp.floor(c0 * (1.0 / 128.0))
     tile1 = jnp.floor(c1 * (1.0 / 128.0))
-    in0 = c0 - 128.0 * tile0 - 1.0
-    idx0 = jnp.maximum(in0, 0.0).astype(jnp.int32)
     idx1 = (c1 - 128.0 * tile1).astype(jnp.int32)
-    some = in0 >= 0.0
+    first = iota((SROWS, 128), 1) == 0
+
+    def less_previous(ends):
+        return ends - jnp.where(first, 0.0, pltpu.roll(ends, 1, 1))
+
     middle = 0.5 * (c0 + c1)
 
     def row_sums(k, carry):
@@ -394,24 +405,20 @@
         sums = list(sums)
         for lt in range(8):
             tile = (k * 8 + lt).astype(F32)
-            last1, last0 = tile1 == tile, tile0 == tile
-            over1, over0 = tile1 > tile, tile0 > tile
-            diffs = []
+            last1, over1 = tile1 == tile, tile1 > tile
+            upto = []
             for half, at in ((0, 0), (1, 0), (0, 16)):
                 rows = slice(32 * lt + at, 32 * lt + at + 16)
                 a = pre[rows, 128 * half : 128 * half + 128]
                 whole = pre[rows, 128 * half + 256 : 128 * half + 384]
                 g1 = jnp.take_along_axis(a, idx1, axis=1)
-                g0 = jnp.where(some, jnp.take_along_axis(a, idx0, axis=1), 0.0)
-                upto1 = jnp.where(last1, g1, jnp.where(over1, whole, 0.0))
-                upto0 = jnp.where(last0, g0, jnp.where(over0, whole, 0.0))
-                diffs.append(upto1 - upto0)
-            sums[0] = sums[0] + diffs[0]
-            sums[1] = sums[1] + (diffs[1] + (128.0 * tile - middle) * diffs[0])
-            sums[2] = sums[2] + diffs[2]
+                upto.append(jnp.where(last1, g1, jnp.where(over1, whole, 0.0)))
+            diff = less_previous(upto[0])
+            sums[0] = sums[0] + diff
+            sums[1] = sums[1] + (128.0 * tile - middle) * diff
+            sums[2] = sums[2] + upto[1]
+            sums[3] = sums[3] + upto[2]
         return tuple(sums)
-
-    pre1[...] = jnp.zeros_like(pre1)
 
     def pair(m, sums):
         prefix(2 * m, pre0)
@@ -419,8 +426,9 @@
         prefix(2 * m + 1, pre1)
         return edges(2 * m, pre0, sums)
     zero = jnp.zeros((SROWS, 128), F32)
-    sums = lax.fori_loop(0, TILES // 16, pair, (zero, zero, zero))
-    s0, s1, s2 = edges(jnp.int32(TILES // 8 - 1), pre1, sums)
+    sums = lax.fori_loop(0, TILES // 16, pair, (zero, zero, zero, zero))
+    s0, s1, s1_inside, s2 = edges(jnp.int32(TILES // 8 - 1), pre1, sums)
+    s1, s2 = s1 + less_previous(s1_inside), less_previous(s2)
     keep = iota((SROWS, 128), 1) < PER_ROW
     s1 = s1 / (0.5 * (c1 - c0 + 1.0))
     s0, s1, s2 = [jnp.where(keep, v, 0.0) for v in (s0, s1, s2)]
@@ -457,8 +465,8 @@
     lax.fori_loop(1, count, step, 0)
 
 
-def kernel(normf, scale, amp_hbm, seg_hbm, box_hbm, coef_hbm, freq_ref, pamp_ref, meas_hbm, ctab_hbm, rtab_hbm,
-           out_ref, box_ref, coef_ref, meas_ref, amp, seg, ctab, rtab, flat, tabs, rowt, base, pick, roww, colw, pbuf, eb0, eb1, acc, ysc,
+def kernel(normf, amp_hbm, seg_hbm, box_hbm, coef_hbm, freq_ref, pamp_ref, meas_hbm, ctab_hbm, rtab_hbm,
+           out_ref, box_ref, coef_ref, meas_ref, amp, seg, ctab, rtab, flat, tabs, rowt, base, pick, roww, colw, pbuf, wbuf, eb0, eb1, acc, ysc,
            pay, recv, lhs, hs, ms, hpay, hid, left, leftt, gbuf, wst, ulow, tris, pre0, pre1, sbuf, pack,
            got_a, mine_b, got_b, mine_c, got_c, lsem, tsem, osem, ssem, rsem, asem, bsem, csem):
     band = lax.axis_index("band")
@@ -526,9 +534,9 @@
                     small[1].wait()
                     segment_setup(row0, box_ref, coef_ref, seg, flat, tabs, rowt, base, pick)
             before = jnp.maximum(2 * i - 1, 0)
-            fields(j, 2 * i, eb0, amp, seg, rowt, base, roww, colw, pbuf)
+            fields(j, 2 * i, eb0, amp, seg, rowt, base, roww, colw, pbuf, wbuf)
             add_dots(acc, ctab, before, eb1)
-            fields(j, 2 * i + 1, eb1, amp, seg, rowt, base, roww, colw, pbuf)
+            fields(j, 2 * i + 1, eb1, amp, seg, rowt, base, roww, colw, pbuf, wbuf)
             add_dots(acc, ctab, 2 * i, eb0)
             return carry
         lax.fori_loop(0, CHUNKS, forward, 0)
@@ -559,6 +567,8 @@
         each(PEERS, one)
         hid[j, me] = hpay[j, me]
 
+    prefix_weights(tris)
+    pre1[...] = jnp.zeros_like(pre1)
     for j in range(2):
         def done(o):
             peer = lax.rem(me + o, PEERS)
@@ -568,7 +578,7 @@
         hidden_left(j, hid.at[j], left, leftt)
 
     def back(i, carry):
-        backward(i, leftt, ctab, gbuf, roww, colw, pbuf, wst)
+        backward(i, leftt, ctab, gbuf, wbuf, pbuf, wst)
         return carry
     lax.fori_loop(0, FOLD // BCHUNK, back, 0)
 
@@ -600,7 +610,7 @@
     total = got_b[0]
     for k in range(1, CHIPS):
         total = total + got_b[k]
-    mine_c[...] = total * scale
+    mine_c[...] = total
 
     def share_copy(o, slot):
         peer = lax.rem(band + o, YS)
@@ -629,8 +639,8 @@
 
     def body(amplitude, seg_map, seg_box, seg_coeffs, probe_freq, probe_amp, measured):
         dma = pltpu.SemaphoreType.DMA
-        return pl.pallas_call(
-            functools.partial(kernel, 1.0 / root, 2.0 / root / (BANDS * PROBES)),
+        sums = pl.pallas_call(
+            functools.partial(kernel, 1.0 / root),
             in_specs=[HBM, HBM, HBM, HBM, SM, SM, HBM, HBM, HBM],
             out_specs=VM,
             out_shape=jax.ShapeDtypeStruct((3, SEG), F32),
@@ -650,6 +660,7 @@
                 pltpu.VMEM((4, ROWS, 128), F32),
                 pltpu.VMEM((4, TILES, 128), F32),
                 pltpu.VMEM((2, ROWS, NC), F32),
+                pltpu.VMEM((4, ROWS, NC), F32),
                 pltpu.VMEM((512, SUB), BF16),
                 pltpu.VMEM((512, SUB), BF16),
                 pltpu.VMEM((4 * HALF, 256), F32),
@@ -688,6 +699,7 @@
             compiler_params=pltpu.CompilerParams(collective_id=0, has_side_effects=True, vmem_limit_bytes=LIMIT),
             name="gradient",
         )(amplitude, seg_map, seg_box, seg_coeffs, probe_freq, probe_amp, measured, ctable, rtable)
+        return sums * (2.0 / root / (BANDS * PROBES))
 
     in_specs = (P("row", None), P("row", None), P(), P(), P(), P(), P("band", "row", None, None, None))
     return jax.shard_map(body, mesh=mesh, in_specs=in_specs, out_specs=P(), check_vma=False)

time: 63.7 us -> 61.1 us (0.959)
  Pallas kernels: 62.2 us -> 59.6 us
  other arithmetic: 0 us -> 1.34 us
  local copies, waits for them, and re-layouts: 1.34 us -> 0 us
    pallas_call x1, Pallas kernels: 62.2 us -> 59.6 us  [body(): pl.pallas_call(functools.partial(kernel, 1.0 / root), in_specs=[HBM, HBM,...]
    mul x0 -> x1, other arithmetic: none -> 1.34 us  [body(): return sums * (2.0 / root / (BANDS * PROBES))]
    unnamed x1 -> x0, local copies, waits for them, and re-layouts: 1.34 us -> none
where the time goes in v1:
time: 61.1 us; the launch traced here: 60.9 us
  Pallas kernels  59.6 us (98%)
  other arithmetic  1.34 us (2%)
    pallas_call x1, Pallas kernels, body(): pl.pallas_call(functools.partial(kernel, 1.0 / root), in_specs=[HBM, HBM,...  59.6 us
    mul x1, other arithmetic, body(): return sums * (2.0 / root / (BANDS * PROBES))  1.34 us

profile of v1, /device:TPU:0, one launch (start us, length us, event | category | flops | bytes accessed | tf_op | source)
XLA Modules:
  0.0 60.9 jit_solution(6624956191257924074)
XLA Ops:
  0.0 59.6 %gradient.1 = f32[3,1200]{1,0:T(4,128)} custom-call(bf16[64,8192]{1,0:T(8,128)(2,1)} %amp_hbm.1, s32[64,8192]{1,0:T(8,128)} %seg_hbm.1, s32[4,1200]{1,0:T(4,128)} %box_hbm.1, f32[3,1200]{1,0:T(4,128)} %coef_hbm.1, s32[2,2]{1,0:T(2,128)} %freq_ref.1, f32[2]{0:T(128)} %pamp_ref.1, f32[2,8,4,2,256]{4,3,2,1,0:T(2,128)} %meas_hbm.1, ...), custom_call_target="tpu_custom_call" | custom-call | tf_op jit(solution)/shard_map/gradient/pallas_call | solution.py:642
  59.6 1.3 %broadcast_multiply_fusion = f32[3,1200]{1,0:T(4,128)} fusion(f32[3,1200]{1,0:T(4,128)} %gradient.1), kind=kLoop, calls=%fused_computation | loop fusion | flops 3600 | bytes 28800 | tf_op jit(solution)/shard_map/mul | solution.py:702

commit v2 on v1

--- a/solution.py
+++ b/solution.py
@@ -462,7 +462,7 @@
     def step(o, carry):
         fn(o)
         return carry
-    lax.fori_loop(1, count, step, 0)
+    lax.fori_loop(1, count, step, 0, unroll=count < PEERS)
 
 
 def kernel(normf, amp_hbm, seg_hbm, box_hbm, coef_hbm, freq_ref, pamp_ref, meas_hbm, ctab_hbm, rtab_hbm,

time: 61.1 us -> 61 us (level)
  no operation moved by 1% of the time
where the time goes in v2:
time: 61 us; the launch traced here: 60.9 us
  Pallas kernels  59.5 us (98%)
  other arithmetic  1.34 us (2%)
    pallas_call x1, Pallas kernels, body(): pl.pallas_call(functools.partial(kernel, 1.0 / root), in_specs=[HBM, HBM,...  59.5 us
    mul x1, other arithmetic, body(): return sums * (2.0 / root / (BANDS * PROBES))  1.34 us

profile of v2, /device:TPU:0, one launch (start us, length us, event | category | flops | bytes accessed | tf_op | source)
XLA Modules:
  0.0 60.9 jit_solution(5094187216610702251)
XLA Ops:
  0.0 59.5 %gradient.1 = f32[3,1200]{1,0:T(4,128)} custom-call(bf16[64,8192]{1,0:T(8,128)(2,1)} %amp_hbm.1, s32[64,8192]{1,0:T(8,128)} %seg_hbm.1, s32[4,1200]{1,0:T(4,128)} %box_hbm.1, f32[3,1200]{1,0:T(4,128)} %coef_hbm.1, s32[2,2]{1,0:T(2,128)} %freq_ref.1, f32[2]{0:T(128)} %pamp_ref.1, f32[2,8,4,2,256]{4,3,2,1,0:T(2,128)} %meas_hbm.1, ...), custom_call_target="tpu_custom_call" | custom-call | tf_op jit(solution)/shard_map/gradient/pallas_call | solution.py:642
  59.5 1.3 %broadcast_multiply_fusion = f32[3,1200]{1,0:T(4,128)} fusion(f32[3,1200]{1,0:T(4,128)} %gradient.1), kind=kLoop, calls=%fused_computation | loop fusion | flops 3600 | bytes 28800 | tf_op jit(solution)/shard_map/mul | solution.py:702
